TPU v7x, 32 devices: a whole 2x2x4 slice. The times are simulated.
32 devices in a mesh: video: 2 (over x), frame: 4 (over z), head: 4 (over y, core).
Axes of the slice: x: 2, y: 2, z: 4, core: 2. Of those that a mesh axis runs over, the one named last changes fastest.
Arguments:
- query: bfloat16 [12288, 3072], P(('video', 'frame'), 'head'), parts along dimension 0, may hold values from -100 to 100
- keys: bfloat16 [12288, 3072], P(('video', 'frame'), 'head'), parts along dimension 0, may hold values from -4.04 to 4.04
- values: bfloat16 [12288, 3072], P(('video', 'frame'), 'head'), parts along dimension 0, may hold values from -6 to 6
- out_weight: bfloat16 [3072, 3072], P('head'), may hold values from -0.5 to 0.5
- tile_lists: int32 [32, 8], P(('video', 'frame')), parts along dimension 0, may hold values from 0 to 15, as said below
Outputs:
- mixed: bfloat16 [12288, 3072], P(('video', 'frame', 'head')), parts along dimension 0
There are 2 independent parts, one for each index of `video`. A program takes and returns all parts, laid end to end along the dimension named above; an argument that names none is the same for every part. Nothing has to cross between parts.
Inputs may be any that keep to these rules, and one draw needn't show every extreme that they name: `tile_lists`: row t names 8 different tiles; the first is tile t itself, the second lies exactly 1 slabs from tile t's slab, and all lie at most 1 slabs from it (the slab of tile u is u // 4).
All inputs are finite; a program needn't handle non-finite values.
Results may differ from a plain program's by a relative error of at most 0.017.
Values may be sent and summed in bfloat16 or wider, within the bound.
A program may use at most 192 MiB of HBM per device.

v0:
```python
import math

import jax
import jax.numpy as jnp
from jax import lax
from jax.sharding import PartitionSpec as P

HD = 128
TILE = 384


def shifted(block, axis, distance):
    devices = range(lax.axis_size(axis))
    route = [(i - distance, i) for i in devices if i - distance in devices]
    return lax.ppermute(block, axis, route)


def on_device(query, keys, values, out_weight, tile_lists):
    frames = lax.axis_size("frame")
    my_slab = lax.axis_index("frame")
    reach_slabs = min(2, (frames - 2) // 2)
    col_width = query.shape[1]
    heads_here = col_width // HD
    tokens_here = query.shape[0]
    tiles_here = tokens_here // TILE
    listed = tile_lists.shape[1]
    score_scale = 1.0 / math.sqrt(HD)
    slab_store = {0: (keys, values)}
    for offset in [entry for entry in range(-reach_slabs, reach_slabs + 1) if entry != 0]:
        slab_store[offset] = shifted((keys, values), "frame", -offset)
    ordered = [slab_store[offset] for offset in range(-reach_slabs, reach_slabs + 1)]
    key_bank = jnp.stack([entry_pair[0] for entry_pair in ordered]).reshape(
        -1, TILE, heads_here, HD
    )
    value_bank = jnp.stack([entry_pair[1] for entry_pair in ordered]).reshape(
        -1, TILE, heads_here, HD
    )
    local_ids = (
        tile_lists // tiles_here - my_slab + reach_slabs
    ) * tiles_here + tile_lists % tiles_here
    query_blocks = query.reshape(tiles_here, TILE, heads_here, HD)

    def attend(block):
        query_block, id_row = block
        key_block = key_bank[id_row].reshape(listed * TILE, heads_here, HD)
        value_block = value_bank[id_row].reshape(listed * TILE, heads_here, HD)
        scores = (
            jnp.einsum("qhd,khd->hqk", query_block, key_block, preferred_element_type=jnp.float32)
            * score_scale
        )
        row_max = jnp.max(scores, axis=-1, keepdims=True)
        exp_scores = jnp.exp(scores - row_max)
        row_total = jnp.sum(exp_scores, axis=-1, keepdims=True)
        weights = exp_scores.astype(jnp.bfloat16)
        mixed_block = jnp.einsum(
            "hqk,khd->qhd", weights, value_block, preferred_element_type=jnp.float32
        )
        mixed_block = mixed_block / jnp.transpose(row_total, (1, 0, 2))
        return mixed_block.astype(jnp.bfloat16).reshape(TILE, col_width)

    attended = lax.map(attend, (query_blocks, local_ids)).reshape(tokens_here, col_width)
    return lax.psum_scatter(
        jnp.dot(attended, out_weight, preferred_element_type=jnp.float32).astype(jnp.bfloat16),
        "head",
        scatter_dimension=0,
        tiled=True,
    )


def solution(mesh):
    return jax.shard_map(
        on_device,
        mesh=mesh,
        in_specs=(
            P(("video", "frame"), "head"),
            P(("video", "frame"), "head"),
            P(("video", "frame"), "head"),
            P("head", None),
            P(("video", "frame"), None),
        ),
        out_specs=P(("video", "frame", "head"), None),
        check_vma=False,
    )
```

profile of v0, /device:TPU:0, one launch (start us, length us, event | category | flops | bytes accessed | tf_op | source)
XLA Modules:
  0.0 460.2 jit_solution(12510221702528092186)
XLA Ops:
  28.4 35.1 %collective-permute-done = bf16[1536,768]{1,0:T(8,128)(2,1)} collective-permute-done((bf16[1536,768]{1,0:T(8,128)(2,1)}, bf16[1536,768]{1,0:T(8,128)(2,1)}, u32[]{:S(2)}, u32[]{:S(2)}) %collective-permute-start) | collective-permute-done | bytes 2359328 | tf_op jit(solution)/shard_map/ppermute | solution.py:15
  75.8 15.3 %reshape.49 = bf16[12,384,6,128]{3,2,1,0:T(8,128)(2,1)} reshape(bf16[3,1536,768]{2,1,0:T(8,128)(2,1)} %pad_maximum_fusion) | data formatting | bytes 14155776 | tf_op jit(solution)/shard_map/reshape | solution.py:35
  91.2 21.8 %collective-permute-done.2 = bf16[1536,768]{1,0:T(8,128)(2,1)} collective-permute-done((bf16[1536,768]{1,0:T(8,128)(2,1)}, bf16[1536,768]{1,0:T(8,128)(2,1)}, u32[]{:S(2)}, u32[]{:S(2)}) %collective-permute-start.2) | collective-permute-done | bytes 2359328 | tf_op jit(solution)/shard_map/ppermute | solution.py:15
  124.4 15.2 %reshape.51 = bf16[12,384,6,128]{3,2,1,0:T(8,128)(2,1)} reshape(bf16[3,1536,768]{2,1,0:T(8,128)(2,1)} %pad_maximum_fusion.1) | data formatting | bytes 14155776 | tf_op jit(solution)/shard_map/reshape | solution.py:32
  139.6 224.1 %while.10 = (s32[]{:T(128)}, bf16[4,384,768]{2,1,0:T(8,128)(2,1)}, s32[4,8]{1,0:T(4,128)S(1)}, bf16[12,384,6,128]{3,2,1,0:T(8,128)(2,1)}, bf16[4,384,6,128]{3,1,...) while((s32[]{:T(128)}, bf16[4,384,768]{2,1,0:T(8,128)(2,1)}, s32[4,8]{1,0:T(4,128)S(1)}, ...), condition=%wide.region_3.4_spmd, body=%wide.region_0.3_spmd.sunk | while | flops 3681088000 | bytes 118409456 | solution.py:61
  139.6 7.6 %gather_fusion = bf16[8,384,6,128]{3,2,1,0:T(8,128)(2,1)} fusion(bf16[12,384,6,128]{3,2,1,0:T(8,128)(2,1)} %get-tuple-element.118, s32[1024]{0:T(1024)S(1)} %pad_clamp_fusion.2), kind=kCustom, calls=%fused_computation.1.clone.1 | custom fusion | bytes 9437216 | tf_op jit(solution)/shard_map/while/body/eval_jaxpr/gather | solution.py:45
  147.2 13.6 %multiply_reduce_fusion.2 = (f32[6,384]{1,0:T(8,128)S(1)}, f32[6,384,3072]{2,1,0:T(8,128)}) fusion(bf16[3072,6,128]{2,1,0:T(8,128)(2,1)} %bitcast.50, bf16[4,384,6,128]{3,1,2,0:T(8,128)(2,1)} %get-tuple-element.117, s32[]{:T(128)} %get-tuple-element.106), kind=kOutput, calls=%fused_computation.3.clone.1 | convolution fusion | flops 1826092800 | bytes 35202560 | tf_op jit(solution)/shard_map/while/body/eval_jaxpr/qhd,khd->hqk/dot_general | solution.py:48
  160.8 11.7 %fusion.39 = f32[6,384]{1,0:T(8,128)S(1)} fusion(f32[6,384,3072]{2,1,0:T(8,128)} %get-tuple-element.97, f32[6,384]{1,0:T(8,128)S(1)} %get-tuple-element.98), kind=kLoop, calls=%fused_computation.4.clone.1 | loop fusion | flops 21231360 | bytes 28329984 | tf_op jit(solution)/shard_map/while/body/eval_jaxpr/reduce_sum | solution.py:53
  172.5 7.6 %gather_fusion.1 = bf16[8,384,6,128]{3,2,1,0:T(8,128)(2,1)} fusion(bf16[12,384,6,128]{3,2,1,0:T(8,128)(2,1)} %get-tuple-element.116, s32[1024]{0:T(1024)S(1)} %pad_clamp_fusion.2), kind=kCustom, calls=%fused_computation.clone.1 | custom fusion | bytes 9437216 | tf_op jit(solution)/shard_map/while/body/eval_jaxpr/gather | solution.py:46
  180.1 14.4 %divide_convert_fusion.2 = bf16[384,6,128]{0,2,1:T(8,128)(2,1)S(1)} fusion(f32[6,384,3072]{2,1,0:T(8,128)} %get-tuple-element.97, f32[6,384]{1,0:T(8,128)S(1)} %get-tuple-element.98, bf16[3072,6,128]{2,1,0:T(8,128)(2,1)} %bitcast.51, f32[384,6]{0,1:T(8,128)S(1)} %bitcast.55), kind=kOutput, calls=%fused_computation.13.clone.1 | convolution fusion | flops 1833762816 | bytes 33638400 | tf_op jit(solution)/shard_map/while/body/eval_jaxpr/hqk,khd->qhd/dot_general | solution.py:55
  203.2 13.6 %multiply_reduce_fusion.2 = (f32[6,384]{1,0:T(8,128)S(1)}, f32[6,384,3072]{2,1,0:T(8,128)}) fusion(bf16[3072,6,128]{2,1,0:T(8,128)(2,1)} %bitcast.50, bf16[4,384,6,128]{3,1,2,0:T(8,128)(2,1)} %get-tuple-element.117, s32[]{:T(128)} %get-tuple-element.106), kind=kOutput, calls=%fused_computation.3.clone.1 | convolution fusion | flops 1826092800 | bytes 35202560 | tf_op jit(solution)/shard_map/while/body/eval_jaxpr/qhd,khd->hqk/dot_general | solution.py:48
  216.8 11.7 %fusion.39 = f32[6,384]{1,0:T(8,128)S(1)} fusion(f32[6,384,3072]{2,1,0:T(8,128)} %get-tuple-element.97, f32[6,384]{1,0:T(8,128)S(1)} %get-tuple-element.98), kind=kLoop, calls=%fused_computation.4.clone.1 | loop fusion | flops 21231360 | bytes 28329984 | tf_op jit(solution)/shard_map/while/body/eval_jaxpr/reduce_sum | solution.py:53
  228.5 7.6 %gather_fusion.1 = bf16[8,384,6,128]{3,2,1,0:T(8,128)(2,1)} fusion(bf16[12,384,6,128]{3,2,1,0:T(8,128)(2,1)} %get-tuple-element.116, s32[1024]{0:T(1024)S(1)} %pad_clamp_fusion.2), kind=kCustom, calls=%fused_computation.clone.1 | custom fusion | bytes 9437216 | tf_op jit(solution)/shard_map/while/body/eval_jaxpr/gather | solution.py:46
  236.1 14.4 %divide_convert_fusion.2 = bf16[384,6,128]{0,2,1:T(8,128)(2,1)S(1)} fusion(f32[6,384,3072]{2,1,0:T(8,128)} %get-tuple-element.97, f32[6,384]{1,0:T(8,128)S(1)} %get-tuple-element.98, bf16[3072,6,128]{2,1,0:T(8,128)(2,1)} %bitcast.51, f32[384,6]{0,1:T(8,128)S(1)} %bitcast.55), kind=kOutput, calls=%fused_computation.13.clone.1 | convolution fusion | flops 1833762816 | bytes 33638400 | tf_op jit(solution)/shard_map/while/body/eval_jaxpr/hqk,khd->qhd/dot_general | solution.py:55
  259.3 13.6 %multiply_reduce_fusion.2 = (f32[6,384]{1,0:T(8,128)S(1)}, f32[6,384,3072]{2,1,0:T(8,128)}) fusion(bf16[3072,6,128]{2,1,0:T(8,128)(2,1)} %bitcast.50, bf16[4,384,6,128]{3,1,2,0:T(8,128)(2,1)} %get-tuple-element.117, s32[]{:T(128)} %get-tuple-element.106), kind=kOutput, calls=%fused_computation.3.clone.1 | convolution fusion | flops 1826092800 | bytes 35202560 | tf_op jit(solution)/shard_map/while/body/eval_jaxpr/qhd,khd->hqk/dot_general | solution.py:48
  272.9 11.7 %fusion.39 = f32[6,384]{1,0:T(8,128)S(1)} fusion(f32[6,384,3072]{2,1,0:T(8,128)} %get-tuple-element.97, f32[6,384]{1,0:T(8,128)S(1)} %get-tuple-element.98), kind=kLoop, calls=%fused_computation.4.clone.1 | loop fusion | flops 21231360 | bytes 28329984 | tf_op jit(solution)/shard_map/while/body/eval_jaxpr/reduce_sum | solution.py:53
  284.5 7.6 %gather_fusion.1 = bf16[8,384,6,128]{3,2,1,0:T(8,128)(2,1)} fusion(bf16[12,384,6,128]{3,2,1,0:T(8,128)(2,1)} %get-tuple-element.116, s32[1024]{0:T(1024)S(1)} %pad_clamp_fusion.2), kind=kCustom, calls=%fused_computation.clone.1 | custom fusion | bytes 9437216 | tf_op jit(solution)/shard_map/while/body/eval_jaxpr/gather | solution.py:46
  292.1 14.4 %divide_convert_fusion.2 = bf16[384,6,128]{0,2,1:T(8,128)(2,1)S(1)} fusion(f32[6,384,3072]{2,1,0:T(8,128)} %get-tuple-element.97, f32[6,384]{1,0:T(8,128)S(1)} %get-tuple-element.98, bf16[3072,6,128]{2,1,0:T(8,128)(2,1)} %bitcast.51, f32[384,6]{0,1:T(8,128)S(1)} %bitcast.55), kind=kOutput, calls=%fused_computation.13.clone.1 | convolution fusion | flops 1833762816 | bytes 33638400 | tf_op jit(solution)/shard_map/while/body/eval_jaxpr/hqk,khd->qhd/dot_general | solution.py:55
  315.3 13.6 %multiply_reduce_fusion.2 = (f32[6,384]{1,0:T(8,128)S(1)}, f32[6,384,3072]{2,1,0:T(8,128)}) fusion(bf16[3072,6,128]{2,1,0:T(8,128)(2,1)} %bitcast.50, bf16[4,384,6,128]{3,1,2,0:T(8,128)(2,1)} %get-tuple-element.117, s32[]{:T(128)} %get-tuple-element.106), kind=kOutput, calls=%fused_computation.3.clone.1 | convolution fusion | flops 1826092800 | bytes 35202560 | tf_op jit(solution)/shard_map/while/body/eval_jaxpr/qhd,khd->hqk/dot_general | solution.py:48
  328.9 11.7 %fusion.39 = f32[6,384]{1,0:T(8,128)S(1)} fusion(f32[6,384,3072]{2,1,0:T(8,128)} %get-tuple-element.97, f32[6,384]{1,0:T(8,128)S(1)} %get-tuple-element.98), kind=kLoop, calls=%fused_computation.4.clone.1 | loop fusion | flops 21231360 | bytes 28329984 | tf_op jit(solution)/shard_map/while/body/eval_jaxpr/reduce_sum | solution.py:53
  340.6 7.6 %gather_fusion.1 = bf16[8,384,6,128]{3,2,1,0:T(8,128)(2,1)} fusion(bf16[12,384,6,128]{3,2,1,0:T(8,128)(2,1)} %get-tuple-element.116, s32[1024]{0:T(1024)S(1)} %pad_clamp_fusion.2), kind=kCustom, calls=%fused_computation.clone.1 | custom fusion | bytes 9437216 | tf_op jit(solution)/shard_map/while/body/eval_jaxpr/gather | solution.py:46
  348.2 14.4 %divide_convert_fusion.2 = bf16[384,6,128]{0,2,1:T(8,128)(2,1)S(1)} fusion(f32[6,384,3072]{2,1,0:T(8,128)} %get-tuple-element.97, f32[6,384]{1,0:T(8,128)S(1)} %get-tuple-element.98, bf16[3072,6,128]{2,1,0:T(8,128)(2,1)} %bitcast.51, f32[384,6]{0,1:T(8,128)S(1)} %bitcast.55), kind=kOutput, calls=%fused_computation.13.clone.1 | convolution fusion | flops 1833762816 | bytes 33638400 | tf_op jit(solution)/shard_map/while/body/eval_jaxpr/hqk,khd->qhd/dot_general | solution.py:55
  363.7 12.4 %convolution_convert_fusion = bf16[1536,3072]{1,0:T(8,128)(2,1)} fusion(bf16[1536,768]{1,0:T(8,128)(2,1)} %bitcast.56, bf16[768,3072]{1,0:T(8,128)(2,1)} %param.10), kind=kOutput, calls=%fused_computation.24 | convolution fusion | flops 7252475904 | bytes 16515072 | tf_op jit(solution)/shard_map/dot_general | solution.py:63
  376.1 77.3 %reduce-scatter.2.cloned.1.call-done = bf16[384,3072]{1,0:T(8,128)(2,1)} async-done(((bf16[1536,3072]{1,0:T(8,128)(2,1)}), bf16[384,3072]{1,0:T(8,128)(2,1)}) %reduce-scatter.2.cloned.1.call-update) | async-done | bytes 2359312 | tf_op jit(solution)/shard_map/reduce_scatter | solution.py:62
  (37 shorter events, 72.9 us)
Async XLA Ops:
  6.5 21.9 %copy-start.1 = (s32[4,8]{1,0:T(4,128)S(1)}, s32[4,8]{1,0:T(4,128)}, u32[]{:S(2)}) copy-start(s32[4,8]{1,0:T(4,128)} %param.11) | copy-start | bytes 388
  6.5 446.8 %reduce-scatter.2.cloned.1.call-start = ((), (), s32[]{:S(2)}) async-start(), calls=%async_computation.1 | async-start | bytes 11796480 | tf_op jit(solution)/shard_map/reduce_scatter | solution.py:62
  6.5 57.0 %collective-permute-start = (bf16[1536,768]{1,0:T(8,128)(2,1)}, bf16[1536,768]{1,0:T(8,128)(2,1)}, u32[]{:S(2)}, u32[]{:S(2)}) collective-permute-start(bf16[1536,768]{1,0:T(8,128)(2,1)} %param.9), channel_id=1, source_target_pairs={{0,4},{4,8},{8,12},{1,5},{5,9},{9,13},{2,6},{6,10},{10,14},{3,7},{... | collective-permute-start | bytes 7077896 | tf_op jit(solution)/shard_map/ppermute | solution.py:15
  13.1 56.4 %collective-permute-start.1 = (bf16[1536,768]{1,0:T(8,128)(2,1)}, bf16[1536,768]{1,0:T(8,128)(2,1)}, u32[]{:S(2)}, u32[]{:S(2)}) collective-permute-start(bf16[1536,768]{1,0:T(8,128)(2,1)} %param.9), channel_id=1, source_target_pairs={{4,0},{8,4},{12,8},{5,1},{9,5},{13,9},{6,2},{10,6},{14,10},{7,3},{... | collective-permute-start | bytes 7077896 | tf_op jit(solution)/shard_map/ppermute | solution.py:15
  14.4 98.6 %collective-permute-start.2 = (bf16[1536,768]{1,0:T(8,128)(2,1)}, bf16[1536,768]{1,0:T(8,128)(2,1)}, u32[]{:S(2)}, u32[]{:S(2)}) collective-permute-start(bf16[1536,768]{1,0:T(8,128)(2,1)} %param.8), channel_id=1, source_target_pairs={{0,4},{4,8},{8,12},{1,5},{5,9},{9,13},{2,6},{6,10},{10,14},{3,7},{... | collective-permute-start | bytes 7077896 | tf_op jit(solution)/shard_map/ppermute | solution.py:15
  20.4 98.2 %collective-permute-start.3 = (bf16[1536,768]{1,0:T(8,128)(2,1)}, bf16[1536,768]{1,0:T(8,128)(2,1)}, u32[]{:S(2)}, u32[]{:S(2)}) collective-permute-start(bf16[1536,768]{1,0:T(8,128)(2,1)} %param.8), channel_id=1, source_target_pairs={{4,0},{8,4},{12,8},{5,1},{9,5},{13,9},{6,2},{10,6},{14,10},{7,3},{... | collective-permute-start | bytes 7077896 | tf_op jit(solution)/shard_map/ppermute | solution.py:15
  75.8 42.7 %copy-start = (bf16[1536,768]{1,0:T(8,128)(2,1)S(1)}, bf16[1536,768]{1,0:T(8,128)(2,1)}, u32[]{:S(2)}) copy-start(bf16[1536,768]{1,0:T(8,128)(2,1)} %param.8) | copy-start | bytes 7077892
Sparse Core Ops, SparseCore 0:
  376.2 77.1 reduce-scatter.1
where the time goes:
time: 462 us; the launch traced here: 460 us
  waiting for transfers between devices  146 us (32%)
  matrix products  124 us (27%)
  local copies, waits for them, and re-layouts  103 us (22%)
  other arithmetic  58.9 us (13%)
  starting transfers between devices  15.1 us (3%)
  between operations  13.4 us (3%)
    reduce_scatter x1, waiting for transfers between devices, on_device(): lax.psum_scatter(jnp.dot(attended, out_weight, preferred_element_type=jnp...  77.3 us
    ppermute x4, waiting for transfers between devices, shifted(): return lax.ppermute(block, axis, route)  68.4 us
    dot_general x4, matrix products, attend(): jnp.einsum('hqk,khd->qhd', weights, value_block, preferred_element_type=j...  57.5 us
    dot_general x4, matrix products, attend(): jnp.einsum('qhd,khd->hqk', query_block, key_block, preferred_element_type...  54.5 us
    reduce_sum x4, other arithmetic, attend(): row_total = jnp.sum(exp_scores, axis=-1, keepdims=True)  46.6 us
    gather x4, local copies, waits for them, and re-layouts, attend(): value_block = value_bank[id_row].reshape(listed * TILE, heads_here, HD)  30.5 us
    gather x4, local copies, waits for them, and re-layouts, attend(): key_block = key_bank[id_row].reshape(listed * TILE, heads_here, HD)  30.4 us
    reshape x1, local copies, waits for them, and re-layouts, on_device(): jnp.stack([entry_pair[1] for entry_pair in ordered])  15.3 us
  transfers between devices with their start and end apart: 5, of which 5 were waited for; matrix products, arithmetic and copies ran while one was open for 6% of the time, Pallas kernels for 0%

commit v1 on v0

v1 whole, which is shorter than its diff:
```python
import functools
import math

import jax
import jax.numpy as jnp
from jax import lax
from jax.experimental import pallas as pl
from jax.experimental.pallas import tpu as pltpu
from jax.sharding import PartitionSpec as P

HD = 128
TILE = 384
MESH = pl.DeviceIdType.MESH
EXP2_SCALE = math.log2(math.e) / math.sqrt(HD)


def attention_kernel(
    frames, groups, reach, ids_ref, q_ref, k_hbm, v_hbm, out_ref,
    kbank, vbank, kcur, vcur, att, s0, s1,
    kv_send, kv_recv, own_sem, a_send, a_recv, a_own,
):
    tokens, cols = q_ref.shape
    heads = cols // HD
    tiles = tokens // TILE
    listed = ids_ref.shape[1]
    rows_out = tokens // groups
    owners_per_tile = TILE // rows_out
    slab = lax.axis_index("frame")
    group = lax.axis_index("head")
    offsets = [d for r in range(1, reach + 1) for d in (-r, r)]
    stores = ((k_hbm, kbank), (v_hbm, vbank))

    def exists(d):
        return (slab + d >= 0) & (slab + d < frames)

    def lanes(h):
        return pl.ds(pl.multiple_of(h * HD, HD), HD)

    def send_kv(h, d, kv):
        src, bank = stores[kv]
        return pltpu.make_async_remote_copy(
            src_ref=src.at[:, lanes(h)],
            dst_ref=bank.at[h, pl.ds((reach - d) * tokens, tokens), :],
            send_sem=kv_send.at[h, reach + d, kv],
            recv_sem=kv_recv.at[h, reach - d, kv],
            device_id={"frame": slab + d},
            device_id_type=MESH,
        )

    def recv_kv(h, d, kv):
        src, bank = stores[kv]
        return pltpu.make_async_remote_copy(
            src_ref=src.at[:, lanes(h)],
            dst_ref=bank.at[h, pl.ds((reach + d) * tokens, tokens), :],
            send_sem=kv_send.at[h, reach + d, kv],
            recv_sem=kv_recv.at[h, reach + d, kv],
            device_id={"frame": slab + d},
            device_id_type=MESH,
        )

    def own_kv(h, kv):
        src, bank = stores[kv]
        return pltpu.make_async_copy(
            src.at[:, lanes(h)],
            bank.at[h, pl.ds(reach * tokens, tokens), :],
            own_sem.at[h, kv],
        )

    def send_att(h, owner):
        return pltpu.make_async_remote_copy(
            src_ref=att.at[h, pl.ds(owner * rows_out, rows_out), :],
            dst_ref=out_ref.at[:, lanes(group * heads + h)],
            send_sem=a_send.at[h, owner],
            recv_sem=a_recv.at[h, group],
            device_id={"head": owner},
            device_id_type=MESH,
        )

    def recv_att(h, sender):
        return pltpu.make_async_remote_copy(
            src_ref=att.at[h, pl.ds(0, rows_out), :],
            dst_ref=out_ref.at[:, lanes(sender * heads + h)],
            send_sem=a_send.at[h, sender],
            recv_sem=a_recv.at[h, sender],
            device_id={"head": sender},
            device_id_type=MESH,
        )

    def own_att(h, owner):
        return pltpu.make_async_copy(
            att.at[h, pl.ds(owner * rows_out, rows_out), :],
            out_ref.at[:, lanes(owner * heads + h)],
            a_own.at[h],
        )

    def issue(h):
        for kv in range(2):
            for d in offsets:
                @pl.when(exists(d))
                def _(d=d, kv=kv):
                    send_kv(h, d, kv).start()
            own_kv(h, kv).start()

    barrier = pltpu.get_barrier_semaphore()
    for d in offsets:
        @pl.when(exists(d))
        def _(d=d):
            pl.semaphore_signal(barrier, inc=1, device_id={"frame": slab + d}, device_id_type=MESH)
    for g in range(groups):
        @pl.when(group != g)
        def _(g=g):
            pl.semaphore_signal(barrier, inc=1, device_id={"head": g}, device_id_type=MESH)
    below = jnp.minimum(slab, reach)
    above = jnp.minimum(frames - 1 - slab, reach)
    pl.semaphore_wait(barrier, groups - 1 + below + above)

    issue(0)
    if heads > 1:
        issue(1)
    vcur[:, :, HD:] = jnp.ones((vcur.shape[0], TILE, HD), vcur.dtype)

    def one_head(h, carry):
        for kv in range(2):
            own_kv(h, kv).wait()
            for d in offsets:
                @pl.when(exists(d))
                def _(d=d, kv=kv):
                    recv_kv(h, d, kv).wait_recv()
        for kv in range(2):
            for d in offsets:
                @pl.when(exists(d))
                def _(d=d, kv=kv):
                    send_kv(h, d, kv).wait_send()

        @pl.when(h + 2 < heads)
        def _():
            issue(h + 2)

        for d in [0] + offsets:
            @pl.when(exists(d))
            def _(d=d):
                for tile in range((reach + d) * tiles, (reach + d + 1) * tiles):
                    rows = slice(tile * TILE, (tile + 1) * TILE)
                    kcur[tile] = kbank[h, rows, :]
                    vcur[tile, :, :HD] = vbank[h, rows, :]

        scratch = (s0, s1)

        def score(t, j, tops):
            s_ref = scratch[t % 2]
            q_tile = q_ref[t * TILE:(t + 1) * TILE, lanes(h)]
            s = lax.dot_general(
                q_tile, kcur[ids_ref[t, j]],
                (((1,), (1,)), ((), ())), preferred_element_type=jnp.float32,
            )
            s_ref[:, j * TILE:(j + 1) * TILE] = s
            for c in range(TILE // HD):
                part = s[:, c * HD:(c + 1) * HD]
                tops = part if tops is None else jnp.maximum(tops, part)
            return tops

        tops = None
        for j in range(listed):
            tops = score(0, j, tops)
        for t in range(tiles):
            row_max = jnp.max(tops, axis=1, keepdims=True)
            tops = None
            total = None
            for j in range(listed):
                if t + 1 < tiles:
                    tops = score(t + 1, j, tops)
                s = scratch[t % 2][:, j * TILE:(j + 1) * TILE]
                weights = jnp.exp2((s - row_max) * EXP2_SCALE).astype(jnp.bfloat16)
                term = jnp.dot(weights, vcur[ids_ref[t, j]], preferred_element_type=jnp.float32)
                total = term if total is None else total + term
            att[h, t * TILE:(t + 1) * TILE, :] = (total[:, :HD] / total[:, HD:]).astype(att.dtype)
            for owner in range(t * owners_per_tile, (t + 1) * owners_per_tile):
                @pl.when(group != owner)
                def _(owner=owner):
                    send_att(h, owner).start()

                @pl.when(group == owner)
                def _(owner=owner):
                    own_att(h, owner).start()
        return carry

    lax.fori_loop(0, heads, one_head, 0)

    def finish(h, carry):
        for g in range(groups):
            @pl.when(group != g)
            def _(g=g):
                recv_att(h, g).wait_recv()
                send_att(h, g).wait_send()

            @pl.when(group == g)
            def _(g=g):
                own_att(h, g).wait()
        return carry

    lax.fori_loop(0, heads, finish, 0)


def on_device(query, keys, values, out_weight, tile_lists):
    frames = lax.axis_size("frame")
    groups = lax.axis_size("head")
    my_slab = lax.axis_index("frame")
    reach = min(2, (frames - 2) // 2)
    tokens, cols = query.shape
    heads = cols // HD
    tiles = tokens // TILE
    listed = tile_lists.shape[1]
    rows_out = tokens // groups
    bank_rows = (2 * reach + 1) * tokens
    full_weight = lax.all_gather(out_weight, "head", axis=0, tiled=True)
    ids = (tile_lists // tiles - my_slab + reach) * tiles + tile_lists % tiles
    attended = pl.pallas_call(
        functools.partial(attention_kernel, frames, groups, reach),
        out_shape=jax.ShapeDtypeStruct((rows_out, cols * groups), jnp.bfloat16),
        in_specs=[
            pl.BlockSpec(memory_space=pltpu.SMEM),
            pl.BlockSpec(memory_space=pltpu.VMEM),
            pl.BlockSpec(memory_space=pl.ANY),
            pl.BlockSpec(memory_space=pl.ANY),
        ],
        out_specs=pl.BlockSpec(memory_space=pl.ANY),
        scratch_shapes=[
            pltpu.VMEM((heads, bank_rows, HD), jnp.bfloat16),
            pltpu.VMEM((heads, bank_rows, HD), jnp.bfloat16),
            pltpu.VMEM((bank_rows // TILE, TILE, HD), jnp.bfloat16),
            pltpu.VMEM((bank_rows // TILE, TILE, 2 * HD), jnp.bfloat16),
            pltpu.VMEM((heads, tokens, HD), jnp.bfloat16),
            pltpu.VMEM((TILE, listed * TILE), jnp.float32),
            pltpu.VMEM((TILE, listed * TILE), jnp.float32),
            pltpu.SemaphoreType.DMA((heads, 2 * reach + 1, 2)),
            pltpu.SemaphoreType.DMA((heads, 2 * reach + 1, 2)),
            pltpu.SemaphoreType.DMA((heads, 2)),
            pltpu.SemaphoreType.DMA((heads, groups)),
            pltpu.SemaphoreType.DMA((heads, groups)),
            pltpu.SemaphoreType.DMA((heads,)),
        ],
        compiler_params=pltpu.CompilerParams(
            collective_id=0, has_side_effects=True, vmem_limit_bytes=56 * 1024 * 1024
        ),
        cost_estimate=pl.CostEstimate(
            flops=4 * tokens * listed * TILE * cols,
            bytes_accessed=8 * tokens * cols,
            transcendentals=tokens * listed * TILE * heads,
        ),
    )(ids, query, keys, values)
    return jnp.dot(attended, full_weight, preferred_element_type=jnp.float32).astype(jnp.bfloat16)


def solution(mesh):
    return jax.shard_map(
        on_device,
        mesh=mesh,
        in_specs=(
            P(("video", "frame"), "head"),
            P(("video", "frame"), "head"),
            P(("video", "frame"), "head"),
            P("head", None),
            P(("video", "frame"), None),
        ),
        out_specs=P(("video", "frame", "head"), None),
        check_vma=False,
    )
```

time: 462 us -> 177 us (0.38)
  Pallas kernels: 0 us -> 127 us
  waiting for transfers between devices: 146 us -> 22.9 us
  matrix products: 124 us -> 13.1 us
  local copies, waits for them, and re-layouts: 103 us -> 0.01 us
  other arithmetic: 58.9 us -> 0.59 us
  starting transfers between devices: 15.1 us -> 0.01 us
    pallas_call x0 -> x1, Pallas kernels: none -> 127 us  [on_device(): pl.pallas_call(functools.partial(attention_kernel, frames, groups, reach)...]
    dot_general x9 -> x1, matrix products: 124 us -> 13.1 us  [on_device(): jnp.dot(attended, full_weight, preferred_element_type=jnp.float32)]
    reduce_scatter x1 -> x0, waiting for transfers between devices: 77.3 us -> none  [on_device(): lax.psum_scatter(jnp.dot(attended, out_weight, preferred_element_type=jnp...]
    ppermute x4 -> x0, waiting for transfers between devices: 68.4 us -> none  [shifted(): return lax.ppermute(block, axis, route)]
    gather x8 -> x0, local copies, waits for them, and re-layouts: 60.9 us -> none  [the longest x4 30.5 us: attend(): value_block = value_bank[id_row].reshape(listed * TILE, heads_here, HD)]
    reduce_sum x4 -> x0, other arithmetic: 46.6 us -> none  [attend(): row_total = jnp.sum(exp_scores, axis=-1, keepdims=True)]
    reshape x3 -> x0, local copies, waits for them, and re-layouts: 35.4 us -> none  [the longest x1 15.3 us: on_device(): jnp.stack([entry_pair[1] for entry_pair in ordered])]
    all_gather x0 -> x1, waiting for transfers between devices: none -> 22.2 us  [on_device(): full_weight = lax.all_gather(out_weight, 'head', axis=0, tiled=True)]
  transfers between devices with their start and end apart: 5 -> 1, of which waited for: 5 -> 1; matrix products, arithmetic and copies ran while one was open for 6% -> 0% of each run, Pallas kernels for 0% -> 72%
where the time goes in v1:
time: 177 us
  Pallas kernels  127 us (72%)
  waiting for transfers between devices  22.9 us (13%)
  between operations  13.4 us (8%)
  matrix products  13.1 us (7%)
    pallas_call x1, Pallas kernels, on_device(): pl.pallas_call(functools.partial(attention_kernel, frames, groups, reach)...  127 us
    all_gather x1, waiting for transfers between devices, on_device(): full_weight = lax.all_gather(out_weight, 'head', axis=0, tiled=True)  22.2 us
    dot_general x1, matrix products, on_device(): jnp.dot(attended, full_weight, preferred_element_type=jnp.float32)  13.1 us
  transfers between devices with their start and end apart: 1, of which 1 were waited for; matrix products, arithmetic and copies ran while one was open for 0% of the time, Pallas kernels for 72%

profile of v1, /device:TPU:0, one launch (start us, length us, event | category | flops | bytes accessed | tf_op | source)
XLA Modules:
  0.0 176.9 jit_solution(17144838065130637851)
XLA Ops:
  6.5 0.0 copy-start
  6.5 0.0 all-gather.2.cloned.1.call-start
  6.5 0.7 all-gather.2.cloned.1.call-update
  7.3 0.0 copy-done
  7.3 0.6 fusion.3.ids_ref
  7.9 126.8 %shard_map.55 = bf16[384,3072]{1,0:T(8,128)(2,1)} custom-call(s32[4,8]{1,0:T(4,128)} %fusion.3.ids_ref, bf16[1536,768]{1,0:T(8,128)(2,1)} %q_ref.1, bf16[1536,768]{1,0:T(8,128)(2,1)} %k_hbm.1, bf16[1536,768]{1,0:T(8,128)(2,1)} %v_hbm.1), custom_call_target="tpu_custom_call" | custom-call | flops 14495514624 | bytes 9437184 | tf_op jit(solution)/shard_map/pallas_call | solution.py:217
  134.7 22.2 %all-gather.2.cloned.1.call-done = bf16[3072,3072]{1,0:T(8,128)(2,1)} async-done(((bf16[768,3072]{1,0:T(8,128)(2,1)}), bf16[3072,3072]{1,0:T(8,128)(2,1)}) %all-gather.2.cloned.1.call-update) | async-done | bytes 18874384 | tf_op jit(solution)/shard_map/all_gather | solution.py:215
  157.0 13.1 %convolution_convert_fusion = bf16[384,3072]{1,0:T(8,128)(2,1)} fusion(bf16[384,3072]{1,0:T(8,128)(2,1)} %shard_map.55, bf16[3072,3072]{1,0:T(8,128)(2,1)} %all-gather.2.cloned.1.call-done), kind=kOutput, calls=%fused_computation | convolution fusion | flops 7248936960 | bytes 23592960 | tf_op jit(solution)/shard_map/dot_general | solution.py:251
Async XLA Ops:
  6.5 0.7 copy-start
  6.5 150.4 %all-gather.2.cloned.1.call-start = ((), (), s32[]{:S(2)}) async-start(), calls=%async_computation | async-start | bytes 23592960 | tf_op jit(solution)/shard_map/all_gather | solution.py:215
Sparse Core Ops, SparseCore 0:
  8.9 147.9 all-gather.1

commit v2 on v1

--- a/solution.py
+++ b/solution.py
@@ -15,9 +15,10 @@
 
 
 def attention_kernel(
-    frames, groups, reach, ids_ref, q_ref, k_hbm, v_hbm, out_ref,
-    kbank, vbank, kcur, vcur, att, s0, s1,
+    frames, groups, videos, reach, ids_ref, q_ref, k_hbm, v_hbm, w_hbm, out_ref,
+    kbank, vbank, kcur, vcur, att, s0, s1, abank, wbank, acc,
     kv_send, kv_recv, own_sem, a_send, a_recv, a_own,
+    w_own, pair_send, pair_recv, row_send, row_recv, spread_send, spread_recv, last_send, last_recv,
 ):
     tokens, cols = q_ref.shape
     heads = cols // HD
@@ -27,6 +28,13 @@
     owners_per_tile = TILE // rows_out
     slab = lax.axis_index("frame")
     group = lax.axis_index("head")
+    video = lax.axis_index("video")
+    core = group % 2
+    row = group // 2
+    rows_of_chips = groups // 2
+    sibling = row * 2 + 1 - core
+    part_rows = HD // videos
+    width = acc.shape[1]
     offsets = [d for r in range(1, reach + 1) for d in (-r, r)]
     stores = ((k_hbm, kbank), (v_hbm, vbank))
 
@@ -69,7 +77,7 @@
     def send_att(h, owner):
         return pltpu.make_async_remote_copy(
             src_ref=att.at[h, pl.ds(owner * rows_out, rows_out), :],
-            dst_ref=out_ref.at[:, lanes(group * heads + h)],
+            dst_ref=abank.at[h, :, lanes(group)],
             send_sem=a_send.at[h, owner],
             recv_sem=a_recv.at[h, group],
             device_id={"head": owner},
@@ -79,7 +87,7 @@
     def recv_att(h, sender):
         return pltpu.make_async_remote_copy(
             src_ref=att.at[h, pl.ds(0, rows_out), :],
-            dst_ref=out_ref.at[:, lanes(sender * heads + h)],
+            dst_ref=abank.at[h, :, lanes(sender)],
             send_sem=a_send.at[h, sender],
             recv_sem=a_recv.at[h, sender],
             device_id={"head": sender},
@@ -89,7 +97,7 @@
     def own_att(h, owner):
         return pltpu.make_async_copy(
             att.at[h, pl.ds(owner * rows_out, rows_out), :],
-            out_ref.at[:, lanes(owner * heads + h)],
+            abank.at[h, :, lanes(owner)],
             a_own.at[h],
         )
 
@@ -101,7 +109,136 @@
                     send_kv(h, d, kv).start()
             own_kv(h, kv).start()
 
+    def own_w(h):
+        return pltpu.make_async_copy(
+            w_hbm.at[pl.ds(pl.multiple_of(h * HD, HD), HD), :],
+            wbank.at[h, pl.ds(pl.multiple_of(group * HD, HD), HD), :],
+            w_own.at[h],
+        )
+
+    def pair_w(h, owner):
+        return pltpu.make_async_remote_copy(
+            src_ref=w_hbm.at[pl.ds(pl.multiple_of(h * HD, HD), HD), :],
+            dst_ref=wbank.at[h, pl.ds(pl.multiple_of(owner * HD, HD), HD), :],
+            send_sem=pair_send.at[h],
+            recv_sem=pair_recv.at[h],
+            device_id={"head": sibling},
+            device_id_type=MESH,
+        )
+
+    def part(owner, piece):
+        return pl.ds(pl.multiple_of(owner * HD + piece * part_rows, part_rows), part_rows)
+
+    def row_w(h, owner, other_row):
+        return pltpu.make_async_remote_copy(
+            src_ref=w_hbm.at[pl.ds(pl.multiple_of(h * HD + video * part_rows, part_rows), part_rows), :],
+            dst_ref=wbank.at[h, part(owner, video), :],
+            send_sem=row_send.at[h, other_row],
+            recv_sem=row_recv.at[h, owner // 2],
+            device_id={"head": other_row * 2 + core},
+            device_id_type=MESH,
+        )
+
+    def spread_w(h, far_row, to_video):
+        owner = far_row * 2 + core
+        return pltpu.make_async_remote_copy(
+            src_ref=wbank.at[h, part(owner, video), :],
+            dst_ref=wbank.at[h, part(owner, video), :],
+            send_sem=spread_send.at[h, far_row, to_video],
+            recv_sem=spread_recv.at[h, far_row, video],
+            device_id={"video": to_video},
+            device_id_type=MESH,
+        )
+
+    def spread_in(h, far_row, from_video):
+        owner = far_row * 2 + core
+        return pltpu.make_async_remote_copy(
+            src_ref=wbank.at[h, part(owner, from_video), :],
+            dst_ref=wbank.at[h, part(owner, from_video), :],
+            send_sem=spread_send.at[h, far_row, from_video],
+            recv_sem=spread_recv.at[h, far_row, from_video],
+            device_id={"video": from_video},
+            device_id_type=MESH,
+        )
+
+    def last_w(h, far_row, piece, owner_core):
+        owner = far_row * 2 + owner_core
+        return pltpu.make_async_remote_copy(
+            src_ref=wbank.at[h, part(owner, piece), :],
+            dst_ref=wbank.at[h, part(owner, piece), :],
+            send_sem=last_send.at[h, far_row, piece],
+            recv_sem=last_recv.at[h, far_row, piece],
+            device_id={"head": sibling},
+            device_id_type=MESH,
+        )
+
+    far_rows = [(row + step) % rows_of_chips for step in range(1, rows_of_chips)]
+    far_videos = [(video + step) % videos for step in range(1, videos)]
+
+    def w_first(h):
+        for far in far_rows:
+            row_w(h, group, far).start()
+        pair_w(h, group).start()
+        own_w(h).start()
+
+    def w_second(h):
+        for far in far_rows:
+            row_w(h, far * 2 + core, far).wait_recv()
+            for other in far_videos:
+                spread_w(h, far, other).start()
+            last_w(h, far, video, core).start()
+
+    def w_third(h):
+        for far in far_rows:
+            for other in far_videos:
+                spread_in(h, far, other).wait_recv()
+                last_w(h, far, other, core).start()
+
+    def w_ready(h):
+        own_w(h).wait()
+        pair_w(h, sibling).wait_recv()
+        for far in far_rows:
+            for piece in range(videos):
+                last_w(h, far, piece, 1 - core).wait_recv()
+
+    def w_sent(h):
+        pair_w(h, group).wait_send()
+        for far in far_rows:
+            row_w(h, group, far).wait_send()
+            for other in far_videos:
+                spread_w(h, far, other).wait_send()
+            for piece in range(videos):
+                last_w(h, far, piece, core).wait_send()
+
+    def rows_ready(h):
+        for g in range(groups):
+            @pl.when(group != g)
+            def _(g=g):
+                recv_att(h, g).wait_recv()
+
+            @pl.when(group == g)
+            def _(g=g):
+                own_att(h, g).wait()
+
+    def project(h, last):
+        w_ready(h)
+        rows_ready(h)
+        step = 512
+
+        def block(b, carry):
+            at = pl.ds(pl.multiple_of(b * step, step), step)
+            term = jnp.dot(abank[h], wbank[h, :, at], preferred_element_type=jnp.float32)
+            if last:
+                out_ref[:, at] = (acc[:, at] + term).astype(out_ref.dtype)
+            else:
+                acc[:, at] += term
+            return carry
+
+        lax.fori_loop(0, width // step, block, 0)
+
     barrier = pltpu.get_barrier_semaphore()
+    for other in far_videos:
+        pl.semaphore_signal(barrier, inc=1, device_id={"video": other}, device_id_type=MESH)
     for d in offsets:
         @pl.when(exists(d))
         def _(d=d):
@@ -112,11 +249,14 @@
             pl.semaphore_signal(barrier, inc=1, device_id={"head": g}, device_id_type=MESH)
     below = jnp.minimum(slab, reach)
     above = jnp.minimum(frames - 1 - slab, reach)
-    pl.semaphore_wait(barrier, groups - 1 + below + above)
+    pl.semaphore_wait(barrier, groups + videos - 2 + below + above)
 
     issue(0)
     if heads > 1:
         issue(1)
+    for first in range(heads):
+        w_first(first)
+    acc[...] = jnp.zeros_like(acc)
     vcur[:, :, HD:] = jnp.ones((vcur.shape[0], TILE, HD), vcur.dtype)
 
     def one_head(h, carry):
@@ -136,6 +276,15 @@
         def _():
             issue(h + 2)
 
+        for chunk in (2 * h, 2 * h + 1):
+            @pl.when(chunk < heads)
+            def _(chunk=chunk):
+                w_second(chunk)
+        for chunk in (2 * h - 2, 2 * h - 1):
+            @pl.when((chunk >= 0) & (chunk < heads))
+            def _(chunk=chunk):
+                w_third(chunk)
+
         for d in [0] + offsets:
             @pl.when(exists(d))
             def _(d=d):
@@ -166,12 +315,14 @@
             row_max = jnp.max(tops, axis=1, keepdims=True)
             tops = None
             total = None
-            for j in range(listed):
+            for j in range(0, listed, 2):
                 if t + 1 < tiles:
                     tops = score(t + 1, j, tops)
-                s = scratch[t % 2][:, j * TILE:(j + 1) * TILE]
+                    tops = score(t + 1, j + 1, tops)
+                s = scratch[t % 2][:, j * TILE:(j + 2) * TILE]
                 weights = jnp.exp2((s - row_max) * EXP2_SCALE).astype(jnp.bfloat16)
-                term = jnp.dot(weights, vcur[ids_ref[t, j]], preferred_element_type=jnp.float32)
+                v_pair = jnp.concatenate([vcur[ids_ref[t, j]], vcur[ids_ref[t, j + 1]]], axis=0)
+                term = jnp.dot(weights, v_pair, preferred_element_type=jnp.float32)
                 total = term if total is None else total + term
             att[h, t * TILE:(t + 1) * TILE, :] = (total[:, :HD] / total[:, HD:]).astype(att.dtype)
             for owner in range(t * owners_per_tile, (t + 1) * owners_per_tile):
@@ -182,20 +333,24 @@
                 @pl.when(group == owner)
                 def _(owner=owner):
                     own_att(h, owner).start()
+
+        @pl.when(h > 0)
+        def _():
+            project(h - 1, False)
+
         return carry
 
     lax.fori_loop(0, heads, one_head, 0)
+    for chunk in range(max(0, 2 * (heads - 1)), heads):
+        w_third(chunk)
+    project(heads - 1, True)
 
     def finish(h, carry):
         for g in range(groups):
             @pl.when(group != g)
             def _(g=g):
-                recv_att(h, g).wait_recv()
                 send_att(h, g).wait_send()
-
-            @pl.when(group == g)
-            def _(g=g):
-                own_att(h, g).wait()
+        w_sent(h)
         return carry
 
     lax.fori_loop(0, heads, finish, 0)
@@ -212,18 +367,21 @@
     listed = tile_lists.shape[1]
     rows_out = tokens // groups
     bank_rows = (2 * reach + 1) * tokens
-    full_weight = lax.all_gather(out_weight, "head", axis=0, tiled=True)
     ids = (tile_lists // tiles - my_slab + reach) * tiles + tile_lists % tiles
-    attended = pl.pallas_call(
-        functools.partial(attention_kernel, frames, groups, reach),
-        out_shape=jax.ShapeDtypeStruct((rows_out, cols * groups), jnp.bfloat16),
+    videos = lax.axis_size("video")
+    chip_rows = groups // 2
+    width = out_weight.shape[1]
+    return pl.pallas_call(
+        functools.partial(attention_kernel, frames, groups, videos, reach),
+        out_shape=jax.ShapeDtypeStruct((rows_out, width), jnp.bfloat16),
         in_specs=[
             pl.BlockSpec(memory_space=pltpu.SMEM),
             pl.BlockSpec(memory_space=pltpu.VMEM),
             pl.BlockSpec(memory_space=pl.ANY),
             pl.BlockSpec(memory_space=pl.ANY),
+            pl.BlockSpec(memory_space=pl.ANY),
         ],
-        out_specs=pl.BlockSpec(memory_space=pl.ANY),
+        out_specs=pl.BlockSpec(memory_space=pltpu.VMEM),
         scratch_shapes=[
             pltpu.VMEM((heads, bank_rows, HD), jnp.bfloat16),
             pltpu.VMEM((heads, bank_rows, HD), jnp.bfloat16),
@@ -232,23 +390,34 @@
             pltpu.VMEM((heads, tokens, HD), jnp.bfloat16),
             pltpu.VMEM((TILE, listed * TILE), jnp.float32),
             pltpu.VMEM((TILE, listed * TILE), jnp.float32),
+            pltpu.VMEM((heads, rows_out, groups * HD), jnp.bfloat16),
+            pltpu.VMEM((heads, groups * HD, width), jnp.bfloat16),
+            pltpu.VMEM((rows_out, width), jnp.float32),
             pltpu.SemaphoreType.DMA((heads, 2 * reach + 1, 2)),
             pltpu.SemaphoreType.DMA((heads, 2 * reach + 1, 2)),
             pltpu.SemaphoreType.DMA((heads, 2)),
             pltpu.SemaphoreType.DMA((heads, groups)),
             pltpu.SemaphoreType.DMA((heads, groups)),
             pltpu.SemaphoreType.DMA((heads,)),
+            pltpu.SemaphoreType.DMA((heads,)),
+            pltpu.SemaphoreType.DMA((heads,)),
+            pltpu.SemaphoreType.DMA((heads,)),
+            pltpu.SemaphoreType.DMA((heads, chip_rows)),
+            pltpu.SemaphoreType.DMA((heads, chip_rows)),
+            pltpu.SemaphoreType.DMA((heads, chip_rows, videos)),
+            pltpu.SemaphoreType.DMA((heads, chip_rows, videos)),
+            pltpu.SemaphoreType.DMA((heads, chip_rows, videos)),
+            pltpu.SemaphoreType.DMA((heads, chip_rows, videos)),
         ],
         compiler_params=pltpu.CompilerParams(
-            collective_id=0, has_side_effects=True, vmem_limit_bytes=56 * 1024 * 1024
+            collective_id=0, has_side_effects=True, vmem_limit_bytes=62 * 1024 * 1024
         ),
         cost_estimate=pl.CostEstimate(
             flops=4 * tokens * listed * TILE * cols,
             bytes_accessed=8 * tokens * cols,
             transcendentals=tokens * listed * TILE * heads,
         ),
-    )(ids, query, keys, values)
-    return jnp.dot(attended, full_weight, preferred_element_type=jnp.float32).astype(jnp.bfloat16)
+    )(ids, query, keys, values, out_weight)
 
 
 def solution(mesh):

time: 177 us -> 129 us (0.73)
  waiting for transfers between devices: 22.9 us -> 0 us
  between operations: 13.4 us -> 0.01 us
  matrix products: 13.1 us -> 0 us
  local copies, waits for them, and re-layouts: 0.01 us -> 3.22 us
  Pallas kernels: 127 us -> 125 us
    all_gather x1 -> x0, waiting for transfers between devices: 22.2 us -> none  [on_device(): full_weight = lax.all_gather(out_weight, 'head', axis=0, tiled=True)]
    dot_general x1 -> x0, matrix products: 13.1 us -> none  [on_device(): jnp.dot(attended, full_weight, preferred_element_type=jnp.float32)]
    unnamed x2 -> x1, local copies, waits for them, and re-layouts: 0.01 us -> 3.22 us
    pallas_call x1, Pallas kernels: 127 us -> 125 us  [on_device(): pl.pallas_call(functools.partial(attention_kernel, frames, groups, videos...]
  transfers between devices with their start and end apart: 1 -> 0, of which waited for: 1 -> 0; matrix products, arithmetic and copies ran while one was open for 0% -> 0% of each run, Pallas kernels for 72% -> 0%
where the time goes in v2:
time: 129 us
  Pallas kernels  125 us (97%)
  local copies, waits for them, and re-layouts  3.22 us (2%)
    pallas_call x1, Pallas kernels, on_device(): pl.pallas_call(functools.partial(attention_kernel, frames, groups, videos...  125 us
    unnamed x1, local copies, waits for them, and re-layouts  3.22 us

profile of v2, /device:TPU:0, one launch (start us, length us, event | category | flops | bytes accessed | tf_op | source)
XLA Modules:
  0.0 129.1 jit_solution(8254858009360962757)
XLA Ops:
  0.0 1.3 fusion.3.ids_ref
  1.3 124.6 %shard_map.55 = bf16[384,3072]{1,0:T(8,128)(2,1)} custom-call(s32[4,8]{1,0:T(4,128)} %fusion.3.ids_ref, bf16[1536,768]{1,0:T(8,128)(2,1)} %q_ref.1, bf16[1536,768]{1,0:T(8,128)(2,1)} %k_hbm.1, bf16[1536,768]{1,0:T(8,128)(2,1)} %v_hbm.1, bf16[768,3072]{1,0:T(8,128)(2,1)} %w_hbm.1), custom_call_target="tpu_custom_call" | custom-call | flops 14495514624 | bytes 9437184 | tf_op jit(solution)/shard_map/pallas_call | solution.py:374
  125.9 3.2 %copy.7 = bf16[384,3072]{1,0:T(8,128)(2,1)} copy(bf16[384,3072]{1,0:T(8,128)(2,1)} %shard_map.55) | data formatting | bytes 4718592

commit v3 on v2

--- a/solution.py
+++ b/solution.py
@@ -15,12 +15,12 @@
 
 
 def attention_kernel(
-    frames, groups, videos, reach, ids_ref, q_ref, k_hbm, v_hbm, w_hbm, out_ref,
-    kbank, vbank, kcur, vcur, att, s0, s1, abank, wbank, acc,
+    frames, groups, videos, reach, ids_ref, q_hbm, k_hbm, v_hbm, w_hbm, out_ref,
+    q_ref, q_sem, kbank, vbank, kcur, vcur, att, s0, s1, abank, wbank, acc,
     kv_send, kv_recv, own_sem, a_send, a_recv, a_own,
     w_own, pair_send, pair_recv, row_send, row_recv, spread_send, spread_recv, last_send, last_recv,
 ):
-    tokens, cols = q_ref.shape
+    tokens, cols = q_hbm.shape
     heads = cols // HD
     tiles = tokens // TILE
     listed = ids_ref.shape[1]
@@ -47,7 +47,7 @@
     def send_kv(h, d, kv):
         src, bank = stores[kv]
         return pltpu.make_async_remote_copy(
-            src_ref=src.at[:, lanes(h)],
+            src_ref=bank.at[h, pl.ds(reach * tokens, tokens), :],
             dst_ref=bank.at[h, pl.ds((reach - d) * tokens, tokens), :],
             send_sem=kv_send.at[h, reach + d, kv],
             recv_sem=kv_recv.at[h, reach - d, kv],
@@ -58,7 +58,7 @@
     def recv_kv(h, d, kv):
         src, bank = stores[kv]
         return pltpu.make_async_remote_copy(
-            src_ref=src.at[:, lanes(h)],
+            src_ref=bank.at[h, pl.ds(reach * tokens, tokens), :],
             dst_ref=bank.at[h, pl.ds((reach + d) * tokens, tokens), :],
             send_sem=kv_send.at[h, reach + d, kv],
             recv_sem=kv_recv.at[h, reach + d, kv],
@@ -103,11 +103,11 @@
 
     def issue(h):
         for kv in range(2):
+            own_kv(h, kv).wait()
             for d in offsets:
                 @pl.when(exists(d))
                 def _(d=d, kv=kv):
                     send_kv(h, d, kv).start()
-            own_kv(h, kv).start()
 
     def own_w(h):
         return pltpu.make_async_copy(
@@ -235,6 +235,10 @@
             return carry
 
         lax.fori_loop(0, width // step, block, 0)
+
+    for early in range(heads):
+        for kv in range(2):
+            own_kv(early, kv).start()
 
     barrier = pltpu.get_barrier_semaphore()
     for other in far_videos:
@@ -254,18 +258,53 @@
     issue(0)
     if heads > 1:
         issue(1)
+    q_load = pltpu.make_async_copy(q_hbm, q_ref, q_sem)
+    q_load.start()
     for first in range(heads):
         w_first(first)
     acc[...] = jnp.zeros_like(acc)
     vcur[:, :, HD:] = jnp.ones((vcur.shape[0], TILE, HD), vcur.dtype)
 
+    q_load.wait()
+    first_id = (reach - slab) * tiles
+
+    def listed_tile(t, j):
+        return jnp.clip(ids_ref[t, j] + first_id, 0, kcur.shape[0] - 1)
+
     def one_head(h, carry):
-        for kv in range(2):
-            own_kv(h, kv).wait()
-            for d in offsets:
-                @pl.when(exists(d))
-                def _(d=d, kv=kv):
-                    recv_kv(h, d, kv).wait_recv()
+        for d in offsets:
+            @pl.when(exists(d))
+            def _(d=d):
+                recv_kv(h, d, 0).wait_recv()
+        for d in [0] + offsets:
+            @pl.when(exists(d))
+            def _(d=d):
+                for tile in range((reach + d) * tiles, (reach + d + 1) * tiles):
+                    kcur[tile] = kbank[h, tile * TILE:(tile + 1) * TILE, :]
+
+        scratch = (s0, s1)
+
+        def score(t, j, tops):
+            s_ref = scratch[t % 2]
+            q_tile = q_ref[t * TILE:(t + 1) * TILE, lanes(h)]
+            s = lax.dot_general(
+                q_tile, kcur[listed_tile(t, j)],
+                (((1,), (1,)), ((), ())), preferred_element_type=jnp.float32,
+            )
+            s_ref[:, j * TILE:(j + 1) * TILE] = s
+            for c in range(TILE // HD):
+                part = s[:, c * HD:(c + 1) * HD]
+                tops = part if tops is None else jnp.maximum(tops, part)
+            return tops
+
+        tops = None
+        for j in range(listed):
+            tops = score(0, j, tops)
+
+        for d in offsets:
+            @pl.when(exists(d))
+            def _(d=d):
+                recv_kv(h, d, 1).wait_recv()
         for kv in range(2):
             for d in offsets:
                 @pl.when(exists(d))
@@ -289,28 +328,8 @@
             @pl.when(exists(d))
             def _(d=d):
                 for tile in range((reach + d) * tiles, (reach + d + 1) * tiles):
-                    rows = slice(tile * TILE, (tile + 1) * TILE)
-                    kcur[tile] = kbank[h, rows, :]
-                    vcur[tile, :, :HD] = vbank[h, rows, :]
-
-        scratch = (s0, s1)
-
-        def score(t, j, tops):
-            s_ref = scratch[t % 2]
-            q_tile = q_ref[t * TILE:(t + 1) * TILE, lanes(h)]
-            s = lax.dot_general(
-                q_tile, kcur[ids_ref[t, j]],
-                (((1,), (1,)), ((), ())), preferred_element_type=jnp.float32,
-            )
-            s_ref[:, j * TILE:(j + 1) * TILE] = s
-            for c in range(TILE // HD):
-                part = s[:, c * HD:(c + 1) * HD]
-                tops = part if tops is None else jnp.maximum(tops, part)
-            return tops
-
-        tops = None
-        for j in range(listed):
-            tops = score(0, j, tops)
+                    vcur[tile, :, :HD] = vbank[h, tile * TILE:(tile + 1) * TILE, :]
+
         for t in range(tiles):
             row_max = jnp.max(tops, axis=1, keepdims=True)
             tops = None
@@ -321,7 +340,7 @@
                     tops = score(t + 1, j + 1, tops)
                 s = scratch[t % 2][:, j * TILE:(j + 2) * TILE]
                 weights = jnp.exp2((s - row_max) * EXP2_SCALE).astype(jnp.bfloat16)
-                v_pair = jnp.concatenate([vcur[ids_ref[t, j]], vcur[ids_ref[t, j + 1]]], axis=0)
+                v_pair = jnp.concatenate([vcur[listed_tile(t, j)], vcur[listed_tile(t, j + 1)]], axis=0)
                 term = jnp.dot(weights, v_pair, preferred_element_type=jnp.float32)
                 total = term if total is None else total + term
             att[h, t * TILE:(t + 1) * TILE, :] = (total[:, :HD] / total[:, HD:]).astype(att.dtype)
@@ -359,15 +378,12 @@
 def on_device(query, keys, values, out_weight, tile_lists):
     frames = lax.axis_size("frame")
     groups = lax.axis_size("head")
-    my_slab = lax.axis_index("frame")
     reach = min(2, (frames - 2) // 2)
     tokens, cols = query.shape
     heads = cols // HD
-    tiles = tokens // TILE
     listed = tile_lists.shape[1]
     rows_out = tokens // groups
     bank_rows = (2 * reach + 1) * tokens
-    ids = (tile_lists // tiles - my_slab + reach) * tiles + tile_lists % tiles
     videos = lax.axis_size("video")
     chip_rows = groups // 2
     width = out_weight.shape[1]
@@ -376,13 +392,15 @@
         out_shape=jax.ShapeDtypeStruct((rows_out, width), jnp.bfloat16),
         in_specs=[
             pl.BlockSpec(memory_space=pltpu.SMEM),
-            pl.BlockSpec(memory_space=pltpu.VMEM),
+            pl.BlockSpec(memory_space=pl.ANY),
             pl.BlockSpec(memory_space=pl.ANY),
             pl.BlockSpec(memory_space=pl.ANY),
             pl.BlockSpec(memory_space=pl.ANY),
         ],
         out_specs=pl.BlockSpec(memory_space=pltpu.VMEM),
         scratch_shapes=[
+            pltpu.VMEM((tokens, cols), jnp.bfloat16),
+            pltpu.SemaphoreType.DMA,
             pltpu.VMEM((heads, bank_rows, HD), jnp.bfloat16),
             pltpu.VMEM((heads, bank_rows, HD), jnp.bfloat16),
             pltpu.VMEM((bank_rows // TILE, TILE, HD), jnp.bfloat16),
@@ -417,7 +435,7 @@
             bytes_accessed=8 * tokens * cols,
             transcendentals=tokens * listed * TILE * heads,
         ),
-    )(ids, query, keys, values, out_weight)
+    )(tile_lists, query, keys, values, out_weight)
 
 
 def solution(mesh):

time: 129 us -> 126 us (0.977)
  Pallas kernels: 125 us -> 122 us
    pallas_call x1, Pallas kernels: 125 us -> 122 us  [on_device(): pl.pallas_call(functools.partial(attention_kernel, frames, groups, videos...]
where the time goes in v3:
time: 126 us
  Pallas kernels  122 us (97%)
  local copies, waits for them, and re-layouts  3.22 us (3%)
    pallas_call x1, Pallas kernels, on_device(): pl.pallas_call(functools.partial(attention_kernel, frames, groups, videos...  122 us
    unnamed x1, local copies, waits for them, and re-layouts  3.22 us

profile of v3, /device:TPU:0, one launch (start us, length us, event | category | flops | bytes accessed | tf_op | source)
XLA Modules:
  0.0 125.6 jit_solution(7283833609277727115)
XLA Ops:
  0.0 122.4 %shard_map.55 = bf16[384,3072]{1,0:T(8,128)(2,1)} custom-call(s32[4,8]{1,0:T(4,128)} %ids_ref.1, bf16[1536,768]{1,0:T(8,128)(2,1)} %q_hbm.1, bf16[1536,768]{1,0:T(8,128)(2,1)} %k_hbm.1, bf16[1536,768]{1,0:T(8,128)(2,1)} %v_hbm.1, bf16[768,3072]{1,0:T(8,128)(2,1)} %w_hbm.1), custom_call_target="tpu_custom_call" | custom-call | flops 14495514624 | bytes 9437184 | tf_op jit(solution)/shard_map/pallas_call | solution.py:390
  122.4 3.2 %copy.7 = bf16[384,3072]{1,0:T(8,128)(2,1)} copy(bf16[384,3072]{1,0:T(8,128)(2,1)} %shard_map.55) | data formatting | bytes 4718592

commit v4 on v3

--- a/solution.py
+++ b/solution.py
@@ -16,7 +16,7 @@
 
 def attention_kernel(
     frames, groups, videos, reach, ids_ref, q_hbm, k_hbm, v_hbm, w_hbm, out_ref,
-    q_ref, q_sem, kbank, vbank, kcur, vcur, att, s0, s1, abank, wbank, acc,
+    q_ref, q_sem, kbank, vbank, kcur, vcur, att, pbank, tops, abank, wbank, acc,
     kv_send, kv_recv, own_sem, a_send, a_recv, a_own,
     w_own, pair_send, pair_recv, row_send, row_recv, spread_send, spread_recv, last_send, last_recv,
 ):
@@ -101,13 +101,12 @@
             a_own.at[h],
         )
 
-    def issue(h):
-        for kv in range(2):
-            own_kv(h, kv).wait()
-            for d in offsets:
-                @pl.when(exists(d))
-                def _(d=d, kv=kv):
-                    send_kv(h, d, kv).start()
+    def issue(h, kv):
+        own_kv(h, kv).wait()
+        for d in offsets:
+            @pl.when(exists(d))
+            def _(d=d):
+                send_kv(h, d, kv).start()
 
     def own_w(h):
         return pltpu.make_async_copy(
@@ -255,9 +254,8 @@
     above = jnp.minimum(frames - 1 - slab, reach)
     pl.semaphore_wait(barrier, groups + videos - 2 + below + above)
 
-    issue(0)
-    if heads > 1:
-        issue(1)
+    issue(0, 0)
+    issue(0, 1)
     q_load = pltpu.make_async_copy(q_hbm, q_ref, q_sem)
     q_load.start()
     for first in range(heads):
@@ -282,38 +280,30 @@
                 for tile in range((reach + d) * tiles, (reach + d + 1) * tiles):
                     kcur[tile] = kbank[h, tile * TILE:(tile + 1) * TILE, :]
 
-        scratch = (s0, s1)
-
-        def score(t, j, tops):
-            s_ref = scratch[t % 2]
+        @pl.when(h + 1 < heads)
+        def _():
+            issue(h + 1, 0)
+
+        for t in range(tiles):
             q_tile = q_ref[t * TILE:(t + 1) * TILE, lanes(h)]
-            s = lax.dot_general(
-                q_tile, kcur[listed_tile(t, j)],
-                (((1,), (1,)), ((), ())), preferred_element_type=jnp.float32,
-            )
-            s_ref[:, j * TILE:(j + 1) * TILE] = s
-            for c in range(TILE // HD):
-                part = s[:, c * HD:(c + 1) * HD]
-                tops = part if tops is None else jnp.maximum(tops, part)
-            return tops
-
-        tops = None
-        for j in range(listed):
-            tops = score(0, j, tops)
+            for i in range(listed // 2):
+                k_pair = jnp.concatenate([kcur[listed_tile(t, 2 * i)], kcur[listed_tile(t, 2 * i + 1)]], axis=0)
+                s = lax.dot_general(
+                    q_tile, k_pair, (((1,), (1,)), ((), ())), preferred_element_type=jnp.float32
+                )
+                top = jnp.max(s, axis=1, keepdims=True)
+                weights = jnp.exp2((s - top) * EXP2_SCALE).astype(jnp.bfloat16)
+                pbank[t, :, 2 * i * TILE:2 * (i + 1) * TILE] = weights
+                tops[t, i] = jnp.broadcast_to(top, (TILE, HD))
 
         for d in offsets:
             @pl.when(exists(d))
             def _(d=d):
                 recv_kv(h, d, 1).wait_recv()
-        for kv in range(2):
-            for d in offsets:
-                @pl.when(exists(d))
-                def _(d=d, kv=kv):
-                    send_kv(h, d, kv).wait_send()
-
-        @pl.when(h + 2 < heads)
+
+        @pl.when(h + 1 < heads)
         def _():
-            issue(h + 2)
+            issue(h + 1, 1)
 
         for chunk in (2 * h, 2 * h + 1):
             @pl.when(chunk < heads)
@@ -331,19 +321,19 @@
                     vcur[tile, :, :HD] = vbank[h, tile * TILE:(tile + 1) * TILE, :]
 
         for t in range(tiles):
-            row_max = jnp.max(tops, axis=1, keepdims=True)
-            tops = None
-            total = None
-            for j in range(0, listed, 2):
-                if t + 1 < tiles:
-                    tops = score(t + 1, j, tops)
-                    tops = score(t + 1, j + 1, tops)
-                s = scratch[t % 2][:, j * TILE:(j + 2) * TILE]
-                weights = jnp.exp2((s - row_max) * EXP2_SCALE).astype(jnp.bfloat16)
-                v_pair = jnp.concatenate([vcur[listed_tile(t, j)], vcur[listed_tile(t, j + 1)]], axis=0)
-                term = jnp.dot(weights, v_pair, preferred_element_type=jnp.float32)
-                total = term if total is None else total + term
-            att[h, t * TILE:(t + 1) * TILE, :] = (total[:, :HD] / total[:, HD:]).astype(att.dtype)
+            pairs = range(listed // 2)
+            row_max = functools.reduce(jnp.maximum, [tops[t, i] for i in pairs])
+            mixed = 0.0
+            row_total = 0.0
+            for i in pairs:
+                v_pair = jnp.concatenate([vcur[listed_tile(t, 2 * i)], vcur[listed_tile(t, 2 * i + 1)]], axis=0)
+                term = jnp.dot(
+                    pbank[t, :, 2 * i * TILE:2 * (i + 1) * TILE], v_pair, preferred_element_type=jnp.float32
+                )
+                share = jnp.exp2((tops[t, i] - row_max) * EXP2_SCALE)
+                mixed = mixed + term[:, :HD] * share
+                row_total = row_total + term[:, HD:] * share
+            att[h, t * TILE:(t + 1) * TILE, :] = (mixed / row_total).astype(att.dtype)
             for owner in range(t * owners_per_tile, (t + 1) * owners_per_tile):
                 @pl.when(group != owner)
                 def _(owner=owner):
@@ -369,6 +359,11 @@
             @pl.when(group != g)
             def _(g=g):
                 send_att(h, g).wait_send()
+        for kv in range(2):
+            for d in offsets:
+                @pl.when(exists(d))
+                def _(d=d, kv=kv):
+                    send_kv(h, d, kv).wait_send()
         w_sent(h)
         return carry
 
@@ -406,8 +401,8 @@
             pltpu.VMEM((bank_rows // TILE, TILE, HD), jnp.bfloat16),
             pltpu.VMEM((bank_rows // TILE, TILE, 2 * HD), jnp.bfloat16),
             pltpu.VMEM((heads, tokens, HD), jnp.bfloat16),
-            pltpu.VMEM((TILE, listed * TILE), jnp.float32),
-            pltpu.VMEM((TILE, listed * TILE), jnp.float32),
+            pltpu.VMEM((tokens // TILE, TILE, listed * TILE), jnp.bfloat16),
+            pltpu.VMEM((tokens // TILE, listed // 2, TILE, HD), jnp.float32),
             pltpu.VMEM((heads, rows_out, groups * HD), jnp.bfloat16),
             pltpu.VMEM((heads, groups * HD, width), jnp.bfloat16),
             pltpu.VMEM((rows_out, width), jnp.float32),

time: 126 us -> 131 us (1.040)
  Pallas kernels: 122 us -> 126 us
    pallas_call x1, Pallas kernels: 122 us -> 126 us  [on_device(): pl.pallas_call(functools.partial(attention_kernel, frames, groups, videos...]
where the time goes in v4:
time: 131 us; the launch traced here: 130 us
  Pallas kernels  126 us (96%)
  local copies, waits for them, and re-layouts  3.22 us (2%)
    pallas_call x1, Pallas kernels, on_device(): pl.pallas_call(functools.partial(attention_kernel, frames, groups, videos...  126 us
    unnamed x1, local copies, waits for them, and re-layouts  3.22 us

profile of v4, /device:TPU:0, one launch (start us, length us, event | category | flops | bytes accessed | tf_op | source)
XLA Modules:
  0.0 129.5 jit_solution(14594945456432071452)
XLA Ops:
  0.0 126.3 %shard_map.55 = bf16[384,3072]{1,0:T(8,128)(2,1)} custom-call(s32[4,8]{1,0:T(4,128)} %ids_ref.1, bf16[1536,768]{1,0:T(8,128)(2,1)} %q_hbm.1, bf16[1536,768]{1,0:T(8,128)(2,1)} %k_hbm.1, bf16[1536,768]{1,0:T(8,128)(2,1)} %v_hbm.1, bf16[768,3072]{1,0:T(8,128)(2,1)} %w_hbm.1), custom_call_target="tpu_custom_call" | custom-call | flops 14495514624 | bytes 9437184 | tf_op jit(solution)/shard_map/pallas_call | solution.py:385
  126.3 3.2 %copy.7 = bf16[384,3072]{1,0:T(8,128)(2,1)} copy(bf16[384,3072]{1,0:T(8,128)(2,1)} %shard_map.55) | data formatting | bytes 4718592

commit v5 on v3

--- a/solution.py
+++ b/solution.py
@@ -101,9 +101,17 @@
             a_own.at[h],
         )
 
-    def issue(h):
+    def sent(h, kv):
+        for d in offsets:
+            @pl.when(exists(d))
+            def _(d=d):
+                send_kv(h, d, kv).wait_send()
+
+    def issue(h, after=None):
         for kv in range(2):
             own_kv(h, kv).wait()
+            if after is not None:
+                sent(after, kv)
             for d in offsets:
                 @pl.when(exists(d))
                 def _(d=d, kv=kv):
@@ -256,8 +264,6 @@
     pl.semaphore_wait(barrier, groups + videos - 2 + below + above)
 
     issue(0)
-    if heads > 1:
-        issue(1)
     q_load = pltpu.make_async_copy(q_hbm, q_ref, q_sem)
     q_load.start()
     for first in range(heads):
@@ -266,6 +272,11 @@
     vcur[:, :, HD:] = jnp.ones((vcur.shape[0], TILE, HD), vcur.dtype)
 
     q_load.wait()
+    if heads > 1:
+        issue(1, after=0)
+    else:
+        sent(0, 0)
+        sent(0, 1)
     first_id = (reach - slab) * tiles
 
     def listed_tile(t, j):
@@ -305,11 +316,10 @@
             @pl.when(exists(d))
             def _(d=d):
                 recv_kv(h, d, 1).wait_recv()
-        for kv in range(2):
-            for d in offsets:
-                @pl.when(exists(d))
-                def _(d=d, kv=kv):
-                    send_kv(h, d, kv).wait_send()
+        @pl.when(h > 0)
+        def _():
+            sent(h, 0)
+            sent(h, 1)
 
         @pl.when(h + 2 < heads)
         def _():

time: 126 us -> 126 us (level)
  no operation moved by 1% of the time
where the time goes in v5:
time: 126 us
  Pallas kernels  122 us (97%)
  local copies, waits for them, and re-layouts  3.22 us (3%)
    pallas_call x1, Pallas kernels, on_device(): pl.pallas_call(functools.partial(attention_kernel, frames, groups, videos...  122 us
    unnamed x1, local copies, waits for them, and re-layouts  3.22 us

profile of v5, /device:TPU:0, one launch (start us, length us, event | category | flops | bytes accessed | tf_op | source)
XLA Modules:
  0.0 125.6 jit_solution(15356956271153725071)
XLA Ops:
  0.0 122.4 %shard_map.55 = bf16[384,3072]{1,0:T(8,128)(2,1)} custom-call(s32[4,8]{1,0:T(4,128)} %ids_ref.1, bf16[1536,768]{1,0:T(8,128)(2,1)} %q_hbm.1, bf16[1536,768]{1,0:T(8,128)(2,1)} %k_hbm.1, bf16[1536,768]{1,0:T(8,128)(2,1)} %v_hbm.1, bf16[768,3072]{1,0:T(8,128)(2,1)} %w_hbm.1), custom_call_target="tpu_custom_call" | custom-call | flops 14495514624 | bytes 9437184 | tf_op jit(solution)/shard_map/pallas_call | solution.py:400
  122.4 3.2 %copy.7 = bf16[384,3072]{1,0:T(8,128)(2,1)} copy(bf16[384,3072]{1,0:T(8,128)(2,1)} %shard_map.55) | data formatting | bytes 4718592
